TPU v7x, 256 devices: a whole 4x4x8 slice. The times are simulated.
256 devices in a mesh: replica: 8 (over z), dp: 32 (over x, y, core).
Axes of the slice: x: 4, y: 4, z: 8, core: 2. Of those that a mesh axis runs over, the one named last changes fastest.
Arguments:
- activations: bfloat16 [196608, 4096], P(('replica', 'dp')), may hold values from -60 to 60
- cotangents: bfloat16 [196608, 1024], P(('replica', 'dp')), may hold values from -0.0390625 to 0.0390625
- error_buffer: float32 [32768, 1024], P(('replica', 'dp')), may hold values from -6 to 6
- master_weights: float32 [4096, 1024], P('dp'), may hold values from -0.75 to 0.75
- first_moment: float32 [4096, 1024], P('dp'), may hold values from -4 to 4
- second_moment: float32 [4096, 1024], P('dp'), may hold values from 0.05 to 2
- warm_factor: float32 [2, 64, 512], replicated, may hold values from -6 to 6
Outputs:
- new_weights: float32 [4096, 1024], P('dp')
- new_first: float32 [4096, 1024], P('dp')
- new_second: float32 [4096, 1024], P('dp')
- new_error: float32 [32768, 1024], P(('replica', 'dp'))
- new_factor: float32 [2, 64, 512], replicated
All inputs are finite; a program needn't handle non-finite values.
Results may differ from a plain program's by a relative error of at most 0.0003.
Values may be sent and summed in bfloat16 or wider, within the bound.
A program may use at most 192 MiB of HBM per device.

v0:
```python
import jax
import jax.numpy as jnp
from jax import lax
from jax.sharding import PartitionSpec as P

highest = lax.Precision.HIGHEST
first_decay = 0.9
second_decay = 0.999
learn_rate = 0.01
adam_epsilon = 1e-08
step_count = 10


def adam_update(update, master_weights, first_moment, second_moment):
    new_first = first_decay * first_moment + (1.0 - first_decay) * update
    new_second = second_decay * second_moment + (1.0 - second_decay) * update * update
    first_hat = new_first / (1.0 - first_decay**step_count)
    second_hat = new_second / (1.0 - second_decay**step_count)
    new_weights = master_weights - learn_rate * first_hat / (jnp.sqrt(second_hat) + adam_epsilon)
    return (new_weights, new_first, new_second)


def lower_solve(chol_factor, right_rows):
    return jax.vmap(
        lambda factor_one, rows_one: jax.scipy.linalg.solve_triangular(
            factor_one, rows_one, lower=True
        )
    )(chol_factor, right_rows)


def local(
    activations, cotangents, error_buffer, master_weights, first_moment, second_moment, warm_factor
):
    token_count, feat_total = activations.shape
    kv_total = cotangents.shape[1]
    kv_width = kv_total // 2
    row_total = feat_total // lax.axis_size("dp")
    rank_total = warm_factor.shape[1]
    pod_rows = lax.psum_scatter(
        lax.dot_general(
            activations, cotangents, (((0,), (0,)), ((), ())), preferred_element_type=jnp.float32
        ),
        "dp",
        scatter_dimension=0,
        tiled=True,
    )
    corrected = pod_rows + error_buffer
    split_rows = corrected.reshape(row_total, 2, kv_width)
    p_factor = jnp.einsum("jkc,rjc->jkr", warm_factor, split_rows, precision=highest)
    p_factor = lax.psum(p_factor, "replica")
    block_width = rank_total // 8
    ortho_basis = jnp.zeros_like(p_factor)
    for block_index in range(8):
        first_col = block_index * block_width
        current = p_factor[:, first_col : first_col + block_width, :]
        projections = jnp.einsum("jkr,jbr->jkb", ortho_basis, current, precision=highest)
        gram_block = jnp.einsum("jar,jbr->jab", current, current, precision=highest)
        projections, gram_block = lax.psum((projections, gram_block), "dp")
        residual = current - jnp.einsum("jkb,jkr->jbr", projections, ortho_basis, precision=highest)
        inner_gram = gram_block - jnp.einsum(
            "jka,jkb->jab", projections, projections, precision=highest
        )
        chol_factor = jnp.linalg.cholesky(inner_gram)
        ortho_basis = ortho_basis.at[:, first_col : first_col + block_width, :].set(
            lower_solve(chol_factor, residual)
        )
    factor_part = jnp.einsum("jkr,rjc->jkc", ortho_basis, split_rows, precision=highest)
    factor_mean = lax.psum(factor_part, ("replica", "dp")) / lax.axis_size("replica")
    approx = jnp.einsum("jkr,jkc->rjc", ortho_basis, factor_mean, precision=highest).reshape(
        row_total, kv_total
    )
    new_error = corrected - approx
    new_weights, new_first, new_second = adam_update(
        approx, master_weights, first_moment, second_moment
    )
    return (new_weights, new_first, new_second, new_error, factor_mean)


def solution(mesh):
    placed = (
        P(("replica", "dp"), None),
        P(("replica", "dp"), None),
        P(("replica", "dp"), None),
        P("dp", None),
        P("dp", None),
        P("dp", None),
        P(),
    )
    return jax.shard_map(
        local,
        mesh=mesh,
        in_specs=placed,
        out_specs=(P("dp", None), P("dp", None), P("dp", None), P(("replica", "dp"), None), P()),
        check_vma=False,
    )
```

profile of v0, /device:TPU:1, one launch (start us, length us, event | category | flops | bytes accessed | tf_op | source)
XLA Modules:
  0.0 1516.5 jit_solution(834759868050541120)
XLA Ops:
  7.2 1.4 copy-done
  8.6 13.0 fusion.64
  21.7 125.5 %reduce-scatter.2.cloned.1.call-done = f32[128,1024]{1,0:T(8,128)} async-done(((f32[4096,1024]{1,0:T(8,128)}), f32[128,1024]{1,0:T(8,128)}) %reduce-scatter.2.cloned.1.call-update) | async-done | bytes 524304 | tf_op jit(solution)/shard_map/reduce_scatter | solution.py:39
  147.2 1.1 add.80
  148.3 1.3 convolution_bitcast_fusion
  149.8 67.4 %all-reduce.12.cloned.1.call-done = f32[2,64,128]{2,1,0:T(8,128)} async-done(((f32[2,64,128]{2,1,0:T(8,128)}), f32[2,64,128]{2,1,0:T(8,128)}) %all-reduce.12.cloned.1.call-update) | async-done | bytes 65552 | tf_op jit(solution)/shard_map/psum | solution.py:50
  217.1 0.8 fusion.10
  217.9 0.9 fusion.57
  218.9 123.7 %all-reduce.8 = (f32[2,64,8]{1,2,0:T(8,128)S(1)}, f32[2,8,8]{1,2,0:T(8,128)S(1)}) all-reduce(f32[2,64,8]{1,2,0:T(8,128)S(1)} %fusion.10, f32[2,8,8]{1,2,0:T(8,128)S(1)} %fusion.57), channel_id=1, replica_groups=mesh['replica'=8,'dp'=32] {'dp'}, use_global_device_ids=true, to_apply=%region_3.0 | all-reduce | flops 1152 | bytes 9216 | tf_op jit(solution)/shard_map/psum | solution.py:58
  342.8 1.4 custom-call.20
  344.5 1.3 custom-call.21
  345.8 0.8 convolution_subtract_fusion.14
  346.6 0.2 fusion.19
  346.8 0.9 fusion.54
  347.7 0.8 fusion.7
  348.6 123.8 %all-reduce.7 = (f32[2,64,8]{1,2,0:T(8,128)S(1)}, f32[2,8,8]{1,2,0:T(8,128)S(1)}) all-reduce(f32[2,64,8]{1,2,0:T(8,128)S(1)} %fusion.7, f32[2,8,8]{1,2,0:T(8,128)S(1)} %fusion.54), channel_id=1, replica_groups=mesh['replica'=8,'dp'=32] {'dp'}, use_global_device_ids=true, to_apply=%region_7.0 | all-reduce | flops 1152 | bytes 9216 | tf_op jit(solution)/shard_map/psum | solution.py:58
  472.6 1.4 custom-call.22
  474.3 1.3 custom-call.23
  475.5 0.8 convolution_subtract_fusion.12
  476.4 0.2 convolution_dynamic-update-slice_fusion.6
  476.6 0.9 fusion.51
  477.5 0.9 fusion.49
  478.4 123.8 %all-reduce.6 = (f32[2,64,8]{1,2,0:T(8,128)S(1)}, f32[2,8,8]{1,2,0:T(8,128)S(1)}) all-reduce(f32[2,64,8]{1,2,0:T(8,128)S(1)} %fusion.49, f32[2,8,8]{1,2,0:T(8,128)S(1)} %fusion.51), channel_id=1, replica_groups=mesh['replica'=8,'dp'=32] {'dp'}, use_global_device_ids=true, to_apply=%region_9.0 | all-reduce | flops 1152 | bytes 9216 | tf_op jit(solution)/shard_map/psum | solution.py:58
  602.4 1.4 custom-call.24
  604.1 1.3 custom-call.25
  605.4 0.9 convolution_subtract_fusion.10
  606.3 0.2 convolution_dynamic-update-slice_fusion.5
  606.5 0.9 fusion.47
  607.4 0.9 fusion.45
  608.3 123.8 %all-reduce.5 = (f32[2,64,8]{1,2,0:T(8,128)S(1)}, f32[2,8,8]{1,2,0:T(8,128)S(1)}) all-reduce(f32[2,64,8]{1,2,0:T(8,128)S(1)} %fusion.45, f32[2,8,8]{1,2,0:T(8,128)S(1)} %fusion.47), channel_id=1, replica_groups=mesh['replica'=8,'dp'=32] {'dp'}, use_global_device_ids=true, to_apply=%region_11.0 | all-reduce | flops 1152 | bytes 9216 | tf_op jit(solution)/shard_map/psum | solution.py:58
  732.3 1.4 custom-call.26
  734.0 1.3 custom-call.27
  735.3 0.9 convolution_subtract_fusion.8
  736.2 0.2 convolution_dynamic-update-slice_fusion.4
  736.4 0.9 fusion.43
  737.3 0.9 fusion.41
  738.2 123.8 %all-reduce.4 = (f32[2,64,8]{1,2,0:T(8,128)S(1)}, f32[2,8,8]{1,2,0:T(8,128)S(1)}) all-reduce(f32[2,64,8]{1,2,0:T(8,128)S(1)} %fusion.41, f32[2,8,8]{1,2,0:T(8,128)S(1)} %fusion.43), channel_id=1, replica_groups=mesh['replica'=8,'dp'=32] {'dp'}, use_global_device_ids=true, to_apply=%region_13.0 | all-reduce | flops 1152 | bytes 9216 | tf_op jit(solution)/shard_map/psum | solution.py:58
  862.2 1.4 custom-call.28
  863.9 1.3 custom-call.29
  865.2 0.9 convolution_subtract_fusion.6
  866.0 0.2 convolution_dynamic-update-slice_fusion.3
  866.2 0.9 fusion.39
  867.2 0.9 fusion.37
  868.1 123.8 %all-reduce.3 = (f32[2,64,8]{1,2,0:T(8,128)S(1)}, f32[2,8,8]{1,2,0:T(8,128)S(1)}) all-reduce(f32[2,64,8]{1,2,0:T(8,128)S(1)} %fusion.37, f32[2,8,8]{1,2,0:T(8,128)S(1)} %fusion.39), channel_id=1, replica_groups=mesh['replica'=8,'dp'=32] {'dp'}, use_global_device_ids=true, to_apply=%region_15.0 | all-reduce | flops 1152 | bytes 9216 | tf_op jit(solution)/shard_map/psum | solution.py:58
  992.1 1.4 custom-call.30
  993.8 1.3 custom-call.31
  995.0 0.9 convolution_subtract_fusion.4
  996.1 0.9 fusion.35
  997.0 0.9 fusion.33
  998.0 123.8 %all-reduce.2 = (f32[2,64,8]{1,2,0:T(8,128)S(1)}, f32[2,8,8]{1,2,0:T(8,128)S(1)}) all-reduce(f32[2,64,8]{1,2,0:T(8,128)S(1)} %fusion.33, f32[2,8,8]{1,2,0:T(8,128)S(1)} %fusion.35), channel_id=1, replica_groups=mesh['replica'=8,'dp'=32] {'dp'}, use_global_device_ids=true, to_apply=%region_17.0 | all-reduce | flops 1152 | bytes 9216 | tf_op jit(solution)/shard_map/psum | solution.py:58
  1122.0 1.4 custom-call.32
  1123.7 1.3 custom-call.33
  1124.9 0.9 convolution_subtract_fusion.2
  1126.0 0.9 fusion.31
  1126.9 0.9 fusion.29
  1127.8 124.0 %all-reduce.1 = (f32[2,64,8]{1,2,0:T(8,128)S(1)}, f32[2,8,8]{1,2,0:T(8,128)S(1)}) all-reduce(f32[2,64,8]{1,2,0:T(8,128)S(1)} %fusion.29, f32[2,8,8]{1,2,0:T(8,128)S(1)} %fusion.31), channel_id=1, replica_groups=mesh['replica'=8,'dp'=32] {'dp'}, use_global_device_ids=true, to_apply=%region_19.0 | all-reduce | flops 1152 | bytes 9216 | tf_op jit(solution)/shard_map/psum | solution.py:58
  1252.0 1.4 custom-call.34
  1253.7 1.3 custom-call.35
  1255.0 0.9 convolution_subtract_fusion
  1256.1 1.1 fusion.1
  1257.2 247.6 %all-reduce.14.cloned.1.call-done = f32[2,64,512]{2,1,0:T(8,128)} async-done(((f32[2,64,512]{2,1,0:T(8,128)}), f32[2,64,512]{2,1,0:T(8,128)}) %all-reduce.14.cloned.1.call-update) | async-done | bytes 262160 | tf_op jit(solution)/shard_map/psum | solution.py:68
  1504.9 1.0 broadcast_multiply_fusion
  1505.8 1.0 fusion.65
  1507.1 2.9 divide_subtract_fusion
  (68 shorter events, 4.8 us)
Async XLA Ops:
  7.2 1.4 copy-start
  7.2 140.0 %reduce-scatter.2.cloned.1.call-start = ((), (), s32[]{:S(2)}) async-start(), calls=%async_computation.1 | async-start | bytes 17301504 | tf_op jit(solution)/shard_map/reduce_scatter | solution.py:39
  21.6 125.6 %copy-start.2 = (f32[128,1024]{1,0:T(8,128)S(1)}, f32[128,1024]{1,0:T(8,128)}, u32[]{:S(2)}) copy-start(f32[128,1024]{1,0:T(8,128)} %param.28) | copy-start | bytes 1572868
  21.6 126.7 %copy-start.3 = (f32[2,64,512]{2,1,0:T(8,128)S(1)}, f32[2,64,512]{2,1,0:T(8,128)}, u32[]{:S(2)}) copy-start(f32[2,64,512]{2,1,0:T(8,128)} %param.32) | copy-start | bytes 786436
  21.7 195.5 %all-reduce.12.cloned.1.call-start = ((), (), s32[]{:S(2)}) async-start(), calls=%async_computation.2 | async-start | bytes 131072 | tf_op jit(solution)/shard_map/psum | solution.py:50
  149.7 1355.2 %all-reduce.14.cloned.1.call-start = ((), (), s32[]{:S(2)}) async-start(), calls=%async_computation.3 | async-start | bytes 524288 | tf_op jit(solution)/shard_map/psum | solution.py:68
  1505.8 4.2 copy-start.1
Sparse Core Ops, SparseCore 0:
  21.8 125.4 reduce-scatter.1
  150.1 66.9 all-reduce.11
  1257.4 247.4 all-reduce.13
where the time goes:
time: 1520 us
  blocking collectives  990 us (65%)
  waiting for transfers between devices  441 us (29%)
  matrix products  40.6 us (3%)
  other arithmetic  28.7 us (2%)
    psum x8, blocking collectives, local(): projections, gram_block = lax.psum((projections, gram_block), 'dp')  990 us
    psum x1, waiting for transfers between devices, local(): lax.psum(factor_part, ('replica', 'dp')) / lax.axis_size('replica')  248 us
    reduce_scatter x1, waiting for transfers between devices, local(): lax.psum_scatter(lax.dot_general(activations, cotangents, (((0,), (0,)),...  126 us
    psum x1, waiting for transfers between devices, local(): p_factor = lax.psum(p_factor, 'replica')  67.4 us
  transfers between devices with their start and end apart: 3, of which 3 were waited for; matrix products, arithmetic and copies ran while one was open for 0% of the time, Pallas kernels for 0%

commit v1 on v0

v1 whole, which is shorter than its diff:
```python
import jax
import jax.numpy as jnp
from jax import lax
from jax.experimental import pallas as pl
from jax.experimental.pallas import tpu as pltpu
from jax.sharding import PartitionSpec as P

highest = lax.Precision.HIGHEST
first_decay = 0.9
second_decay = 0.999
learn_rate = 0.01
adam_epsilon = 1e-08
step_count = 10

F32 = jnp.float32
BF16 = jnp.bfloat16
RING = 4
DEPTH = 8
OFFSETS = (2, 1, 3, 0)


def dot_t(a, b):
    return lax.dot_general(a, b, (((1,), (1,)), ((), ())), precision=highest, preferred_element_type=F32)


def dot_n(a, b):
    return jnp.dot(a, b, precision=highest, preferred_element_type=F32)


class Wire:
    def __init__(self, send, recv):
        self.send, self.recv, self.copies = send, recv, []

    def start(self, src, dst, device):
        i = len(self.copies)
        copy = pltpu.make_async_remote_copy(
            src_ref=src, dst_ref=dst, send_sem=self.send.at[i], recv_sem=self.recv.at[i],
            device_id=device, device_id_type=pl.DeviceIdType.MESH,
        )
        copy.start()
        self.copies.append(copy)
        return copy

    def drain(self):
        for copy in self.copies:
            copy.wait_send()


class Local:
    def __init__(self, sems):
        self.sems, self.count = sems, 0

    def start(self, src, dst):
        copy = pltpu.make_async_copy(src, dst, self.sems.at[self.count])
        copy.start()
        self.count += 1
        return copy


def kernel_a(
    acts, cots, err, warm,
    corr_out, pt_out, linv_out, n_out,
    acts_v, cots_v, cots_t, own, rel_a, rel_b, from_m, from_p, rel2_a, rel2_b, from2_m, from2_p,
    err_v, warm_v, m_t, pt_loc, zr, zsum, n_loc, n_rx, g_loc, g_rx, ns, ra, na, rb, nb, zs, nz, na2, ga, gb, g_half, g_all,
    t_mat, send_sem, recv_sem, loc_sem,
):
    z = lax.axis_index("replica")
    dp = lax.axis_index("dp")
    c = dp % 2
    x = dp // 8
    y = (dp // 2) % 4
    p = x * (1 - c) + y * c
    q = y * (1 - c) + x * c
    sa = 8 - 6 * c
    sb = 2 + 6 * c
    tokens = cots.shape[0]

    def at(pp, qq):
        return (z, (pp % 4) * sa + (qq % 4) * sb + c)

    def along_a(k):
        return at(p + k, q)

    def along_b(k):
        return at(p, q + k)

    def along_z(k):
        return ((z + k) % DEPTH, dp)

    partner = (z, dp + 1 - 2 * c)

    def own_cols(t, s):
        d = ((p + OFFSETS[s]) % 4) * sa + ((q + OFFSETS[t]) % 4) * sb + c
        return pl.ds(pl.multiple_of(d * 128, 128), 128)

    def partner_cols(t, s):
        d = ((q + OFFSETS[s]) % 4) * sb + ((p + OFFSETS[t]) % 4) * sa + 1 - c
        return pl.ds(pl.multiple_of(d * 128, 128), 128)

    wire = Wire(send_sem, recv_sem)
    local = Local(loc_sem)

    cots_here = local.start(cots, cots_v.at[0])
    acts_here = [[None] * 4 for _ in range(4)]
    acts_there = [[None] * 4 for _ in range(4)]
    for s in range(4):
        acts_here[0][s] = local.start(acts.at[:, own_cols(0, s)], acts_v.at[0, pl.ds(0, tokens), pl.ds(128 * s, 128)])

    barrier = pltpu.get_barrier_semaphore()
    friends = [partner] + [along_a(k) for k in (1, 2, 3)] + [along_b(k) for k in (1, 2, 3)] + [along_z(k) for k in range(1, DEPTH)]
    for friend in friends:
        pl.semaphore_signal(barrier, inc=1, device_id=friend, device_id_type=pl.DeviceIdType.MESH)
    pl.semaphore_wait(barrier, len(friends))

    cots_there = wire.start(cots, cots_v.at[1], partner)
    for t in range(4):
        for s in range(4):
            if t > 0:
                acts_here[t][s] = local.start(
                    acts.at[:, own_cols(t, s)], acts_v.at[t, pl.ds(0, tokens), pl.ds(128 * s, 128)])
            acts_there[t][s] = wire.start(
                acts.at[:, partner_cols(t, s)], acts_v.at[t, pl.ds(tokens, tokens), pl.ds(128 * s, 128)], partner)
    err_copy = local.start(err, err_v)
    warm_copy = local.start(warm, warm_v)

    def turn(h):
        @pl.loop(0, 8)
        def _(i):
            cols = pl.ds(pl.multiple_of(i * 128, 128), 128)
            cots_t[cols, h * tokens:(h + 1) * tokens] = cots_v[h, :, cols].T

    cots_here.wait()
    turn(0)
    cots_there.wait_recv()
    turn(1)

    def compute(t):
        for s in range(4):
            acts_here[t][s].wait()
            acts_there[t][s].wait_recv()

        @pl.loop(0, 4)
        def _(i):
            rows = pl.ds(pl.multiple_of(i * 256, 256), 256)
            part = jnp.dot(cots_t[rows, :], acts_v[t], preferred_element_type=F32)
            for s in range(4):
                own[t, s, rows, :] = part[:, 128 * s:128 * (s + 1)]

    lo, hi = pl.ds(0, 512), pl.ds(512, 512)
    relay_a, relay_b, outer_m, outer_p, inner_m, inner_p = ([None] * 4 for _ in range(6))

    def send_relay(t):
        relay_a[t] = wire.start(own.at[t, 0, lo], rel_a.at[t], along_a(1))
        relay_b[t] = wire.start(own.at[t, 0, hi], rel_b.at[t], along_a(3))

    def send_outer(t):
        outer_m[t] = wire.start(own.at[t, 1, hi], from_m.at[t, hi], along_a(1))
        outer_p[t] = wire.start(own.at[t, 2, lo], from_p.at[t, lo], along_a(3))

    def send_inner(t):
        relay_a[t].wait_recv()
        own[t, 1, lo, :] += rel_a[t]
        inner_m[t] = wire.start(own.at[t, 1, lo], from_m.at[t, lo], along_a(1))
        relay_b[t].wait_recv()
        own[t, 2, hi, :] += rel_b[t]
        inner_p[t] = wire.start(own.at[t, 2, hi], from_p.at[t, hi], along_a(3))

    def gather(t):
        for copy in (outer_m[t], outer_p[t], inner_m[t], inner_p[t]):
            copy.wait_recv()
        own[t, 3] += from_m[t] + from_p[t]

    compute(0)
    send_relay(0)
    send_outer(0)
    compute(1)
    send_relay(1)
    send_inner(0)
    send_outer(1)
    compute(2)
    send_relay(2)
    send_inner(1)
    send_outer(2)
    gather(0)
    second_a = wire.start(own.at[0, 3, lo], rel2_a, along_b(1))
    second_b = wire.start(own.at[0, 3, hi], rel2_b, along_b(3))
    compute(3)
    send_relay(3)
    send_inner(2)
    send_outer(3)
    gather(1)
    outer2_m = wire.start(own.at[1, 3, hi], from2_m.at[hi], along_b(1))
    second_a.wait_recv()
    own[1, 3, lo, :] += rel2_a[...]
    inner2_m = wire.start(own.at[1, 3, lo], from2_m.at[lo], along_b(1))
    send_inner(3)
    gather(2)
    outer2_p = wire.start(own.at[2, 3, lo], from2_p.at[lo], along_b(3))
    second_b.wait_recv()
    own[2, 3, hi, :] += rel2_b[...]
    inner2_p = wire.start(own.at[2, 3, hi], from2_p.at[hi], along_b(3))

    err_copy.wait()
    for i in range(8):
        m_t[128 * i:128 * (i + 1), :] = err_v[:, 128 * i:128 * (i + 1)].T
    gather(3)
    for copy in (outer2_m, inner2_m, outer2_p, inner2_p):
        copy.wait_recv()
    m_t[...] += own[3, 3] + (from2_m[...] + from2_p[...])

    warm_copy.wait()
    for j in range(2):
        pt_loc[64 * j:64 * (j + 1), :] = dot_n(warm_v[j], m_t[512 * j:512 * (j + 1), :])

    def z_rows(zz):
        return pl.ds(pl.multiple_of((zz % DEPTH) * 16, 16), 16)

    scatter = [wire.start(pt_loc.at[z_rows(z + k)], zr.at[k], along_z(k)) for k in range(1, DEPTH)]
    total = pt_loc[z_rows(z), :]
    for k in range(1, DEPTH):
        scatter[k - 1].wait_recv()
        total = total + zr[k]
    zsum[...] = total
    spread = [wire.start(zsum, pt_out.at[z_rows(z)], along_z(k)) for k in range(1, DEPTH)]
    pt_out[z_rows(z), :] = total
    for i in range(8):
        corr_out[:, 128 * i:128 * (i + 1)] = m_t[128 * i:128 * (i + 1), :].T
    for copy in spread:
        copy.wait_recv()

    pt = pt_out[...]
    lane = lax.broadcasted_iota(jnp.int32, (64, 128), 1)
    gram = dot_t(pt, pt)
    g_loc[...] = jnp.where(lane < 64, gram[0:64], gram[64:128])
    g_swap = wire.start(g_loc, g_rx, partner)
    for j in range(2):
        for i in range(4):
            n_loc[j, 64 * i:64 * (i + 1), :] = dot_t(
                pt[64 * j:64 * (j + 1)], m_t[512 * j + 128 * i:512 * j + 128 * (i + 1), :])
    n_swap = wire.start(n_loc.at[1 - c], n_rx, partner)

    half = pl.ds(pl.multiple_of(c * 32, 32), 32)
    g_swap.wait_recv()
    ga[p] = g_loc[half, :] + g_rx[half, :]
    ga_copies = [wire.start(ga.at[p], ga.at[p], along_a(k)) for k in (1, 2, 3)]

    n_swap.wait_recv()
    ns[...] = n_loc[c] + n_rx[...]

    def rows_of(index, size):
        return pl.ds(pl.multiple_of((index % 4) * size, size), size)

    ra_copies = [wire.start(ns.at[rows_of(p + k, 64)], ra.at[k], along_a(k)) for k in (1, 2, 3)]
    for copy in ga_copies:
        copy.wait_recv()
    gb[q] = (ga[0] + ga[1]) + (ga[2] + ga[3])
    gb_copies = [wire.start(gb.at[q], gb.at[q], along_b(k)) for k in (1, 2, 3)]
    for copy in ra_copies:
        copy.wait_recv()
    na[...] = (ns[rows_of(p, 64), :] + ra[1]) + (ra[2] + ra[3])
    rb_copies = [wire.start(na.at[rows_of(q + k, 16)], rb.at[k], along_b(k)) for k in (1, 2, 3)]
    for copy in gb_copies:
        copy.wait_recv()
    g_part = (gb[0] + gb[1]) + (gb[2] + gb[3])
    g_half[...] = g_part
    g_all[half, :] = g_part
    g_back = wire.start(g_half, g_all.at[half], partner)
    for copy in rb_copies:
        copy.wait_recv()
    nb[...] = (na[rows_of(q, 16), :] + rb[1]) + (rb[2] + rb[3])
    zs_copies = [wire.start(nb, zs.at[z], along_z(k)) for k in range(1, DEPTH)]
    zs[z] = nb[...]

    g_back.wait_recv()
    row = lax.broadcasted_iota(jnp.int32, (64, 128), 0)
    g = g_all[...]
    eye = jnp.where(lane == row, 1.0, 0.0).astype(F32)
    t_mat[0] = jnp.where(lane >= 64, pltpu.roll(g, 64, 1), eye)
    t_mat[1] = jnp.where(lane >= 64, g, eye)

    def eliminate(first, last):
        for k in range(first, last):
            base = 8 * (k // 8)
            below = lax.broadcasted_iota(jnp.int32, (64 - base, 1), 0) > k - base
            for j in range(2):
                pivot_row = t_mat[j, k:k + 1, :]
                inv = 1.0 / jnp.sqrt(pivot_row[:, 64 + k:65 + k])
                scaled = pivot_row * inv
                column = t_mat[j, base:64, 64 + k:65 + k] * inv
                column = jnp.where(below, column, 0.0)
                t_mat[j, base:64, :] -= column * scaled
                t_mat[j, k:k + 1, :] = scaled

    eliminate(0, 20)
    for copy in zs_copies:
        copy.wait_recv()
    nz[...] = ((zs[0] + zs[1]) + (zs[2] + zs[3])) + ((zs[4] + zs[5]) + (zs[6] + zs[7]))
    back_b = [wire.start(nz, na2.at[rows_of(q, 16)], along_b(k)) for k in (1, 2, 3)]
    na2[rows_of(q, 16), :] = nz[...]
    eliminate(20, 35)
    for copy in back_b:
        copy.wait_recv()
    back_a = [wire.start(na2, n_out.at[c, rows_of(p, 64)], along_a(k)) for k in (1, 2, 3)]
    n_out[c, rows_of(p, 64), :] = na2[...]
    eliminate(35, 50)
    for copy in back_a:
        copy.wait_recv()
    back_c = wire.start(n_out.at[c], n_out.at[c], partner)
    eliminate(50, 64)
    linv_out[...] = t_mat[...]
    back_c.wait_recv()
    wire.drain()


def kernel_b(corr, pt, linv, n, weights, first, second, w_out, first_out, second_out, err_out, factor_out):
    for j in range(2):
        inverse = linv[j][:, 0:64]
        basis = dot_n(inverse, pt[64 * j:64 * (j + 1), :]).T
        for i in range(4):
            cols = slice(512 * j + 128 * i, 512 * j + 128 * (i + 1))
            factor = dot_n(inverse, n[j, 64 * i:64 * (i + 1), :]) * 0.125
            factor_out[j, :, 128 * i:128 * (i + 1)] = factor
            approx = dot_n(basis, factor)
            err_out[:, cols] = corr[:, cols] - approx
            new_first = first_decay * first[:, cols] + (1.0 - first_decay) * approx
            new_second = second_decay * second[:, cols] + (1.0 - second_decay) * approx * approx
            first_out[:, cols] = new_first
            second_out[:, cols] = new_second
            first_hat = new_first / (1.0 - first_decay**step_count)
            second_hat = new_second / (1.0 - second_decay**step_count)
            w_out[:, cols] = weights[:, cols] - learn_rate * first_hat / (jnp.sqrt(second_hat) + adam_epsilon)


def local(activations, cotangents, error_buffer, master_weights, first_moment, second_moment, warm_factor):
    tokens = activations.shape[0]
    rows, cols = error_buffer.shape
    shape = jax.ShapeDtypeStruct
    vmem = pl.BlockSpec(memory_space=pltpu.VMEM)
    anywhere = pl.BlockSpec(memory_space=pl.ANY)
    copies = 120
    corr, pt, linv, n = pl.pallas_call(
        kernel_a,
        out_shape=(shape((rows, cols), F32), shape((128, 128), F32), shape((2, 64, 128), F32), shape((2, 256, 128), F32)),
        in_specs=[anywhere] * 4,
        out_specs=(vmem,) * 4,
        scratch_shapes=[
            pltpu.VMEM((4, 2 * tokens, 512), BF16),
            pltpu.VMEM((2, tokens, cols), BF16),
            pltpu.VMEM((cols, 2 * tokens), BF16),
            pltpu.VMEM((4, 4, cols, 128), F32),
            pltpu.VMEM((4, 512, 128), F32),
            pltpu.VMEM((4, 512, 128), F32),
            pltpu.VMEM((4, cols, 128), F32),
            pltpu.VMEM((4, cols, 128), F32),
            pltpu.VMEM((512, 128), F32),
            pltpu.VMEM((512, 128), F32),
            pltpu.VMEM((cols, 128), F32),
            pltpu.VMEM((cols, 128), F32),
            pltpu.VMEM((rows, cols), F32),
            pltpu.VMEM((2, 64, 512), F32),
            pltpu.VMEM((cols, 128), F32),
            pltpu.VMEM((128, 128), F32),
            pltpu.VMEM((8, 16, 128), F32),
            pltpu.VMEM((16, 128), F32),
            pltpu.VMEM((2, 256, 128), F32),
            pltpu.VMEM((256, 128), F32),
            pltpu.VMEM((64, 128), F32),
            pltpu.VMEM((64, 128), F32),
            pltpu.VMEM((256, 128), F32),
            pltpu.VMEM((4, 64, 128), F32),
            pltpu.VMEM((64, 128), F32),
            pltpu.VMEM((4, 16, 128), F32),
            pltpu.VMEM((16, 128), F32),
            pltpu.VMEM((8, 16, 128), F32),
            pltpu.VMEM((16, 128), F32),
            pltpu.VMEM((64, 128), F32),
            pltpu.VMEM((4, 32, 128), F32),
            pltpu.VMEM((4, 32, 128), F32),
            pltpu.VMEM((32, 128), F32),
            pltpu.VMEM((64, 128), F32),
            pltpu.VMEM((2, 64, 128), F32),
            pltpu.SemaphoreType.DMA((copies,)),
            pltpu.SemaphoreType.DMA((copies,)),
            pltpu.SemaphoreType.DMA((24,)),
        ],
        compiler_params=pltpu.CompilerParams(
            collective_id=0, has_side_effects=True, vmem_limit_bytes=44 * 1024 * 1024),
    )(activations, cotangents, error_buffer, warm_factor)
    tile = shape((rows, cols), F32)
    return pl.pallas_call(
        kernel_b,
        out_shape=(tile, tile, tile, tile, shape(warm_factor.shape, F32)),
        in_specs=[vmem] * 7,
        out_specs=(vmem,) * 5,
        compiler_params=pltpu.CompilerParams(vmem_limit_bytes=16 * 1024 * 1024),
    )(corr, pt, linv, n, master_weights, first_moment, second_moment)


def solution(mesh):
    placed = (
        P(("replica", "dp"), None),
        P(("replica", "dp"), None),
        P(("replica", "dp"), None),
        P("dp", None),
        P("dp", None),
        P("dp", None),
        P(),
    )
    return jax.shard_map(
        local,
        mesh=mesh,
        in_specs=placed,
        out_specs=(P("dp", None), P("dp", None), P("dp", None), P(("replica", "dp"), None), P()),
        check_vma=False,
    )
```

time: 1520 us -> 110 us (0.07)
  blocking collectives: 990 us -> 0 us
  waiting for transfers between devices: 441 us -> 0 us
  Pallas kernels: 0 us -> 103 us
  matrix products: 40.6 us -> 0 us
  other arithmetic: 28.7 us -> 0 us
    psum x8 -> x0, blocking collectives: 990 us -> none  [local(): projections, gram_block = lax.psum((projections, gram_block), 'dp')]
    psum x2 -> x0, waiting for transfers between devices: 315 us -> none  [the longest x1 248 us: local(): lax.psum(factor_part, ('replica', 'dp')) / lax.axis_size('replica')]
    reduce_scatter x1 -> x0, waiting for transfers between devices: 126 us -> none  [local(): lax.psum_scatter(lax.dot_general(activations, cotangents, (((0,), (0,)),...]
    pallas_call x0 -> x2, Pallas kernels: none -> 103 us  [the longest x1 100 us: local(): pl.pallas_call(kernel_a, out_shape=(shape((rows, cols), F32), shape((128,...]
    dot_general x36 -> x0, matrix products: 39 us -> none  [the longest x1 13 us: local(): lax.dot_general(activations, cotangents, (((0,), (0,)), ((), ())), prefer...]
    another operation x42 -> x0, other arithmetic: 23.6 us -> none  [the longest x25 12.9 us: local(): chol_factor = jnp.linalg.cholesky(inner_gram)]
  transfers between devices with their start and end apart: 3 -> 0, of which waited for: 3 -> 0; matrix products, arithmetic and copies ran while one was open for 0% -> 0% of each run, Pallas kernels for 0% -> 0%
where the time goes in v1:
time: 110 us
  Pallas kernels  103 us (94%)
  local copies, waits for them, and re-layouts  6.19 us (6%)
    pallas_call x1, Pallas kernels, local(): pl.pallas_call(kernel_a, out_shape=(shape((rows, cols), F32), shape((128,...  100 us
    unnamed x14, local copies, waits for them, and re-layouts  6.19 us
    pallas_call x1, Pallas kernels, local(): pl.pallas_call(kernel_b, out_shape=(tile, tile, tile, tile, shape(warm_fa...  2.99 us

profile of v1, /device:TPU:1, one launch (start us, length us, event | category | flops | bytes accessed | tf_op | source)
XLA Modules:
  0.0 109.8 jit_solution(17943563740442529531)
XLA Ops:
  0.6 0.0 copy-start
  0.6 2.8 %copy-done = bf16[768,4096]{1,0:T(8,128)(2,1)S(1)} copy-done((bf16[768,4096]{1,0:T(8,128)(2,1)S(1)}, bf16[768,4096]{1,0:T(8,128)(2,1)}, u32[]{:S(2)}) %copy-start) | copy-done | bytes 6291480
  3.4 0.0 copy-start.1
  3.4 1.4 %copy-done.1 = bf16[768,1024]{1,0:T(8,128)(2,1)S(1)} copy-done((bf16[768,1024]{1,0:T(8,128)(2,1)S(1)}, bf16[768,1024]{1,0:T(8,128)(2,1)}, u32[]{:S(2)}) %copy-start.1) | copy-done | bytes 1572888
  4.8 0.0 copy-start.2
  4.8 1.0 copy-done.2
  5.9 0.0 copy-start.6
  5.9 0.9 copy-done.6
  6.8 0.0 copy-start.3
  6.8 0.0 copy-start.4
  6.8 0.0 copy-start.5
  6.8 100.0 %shard_map.110 = (f32[128,1024]{1,0:T(8,128)S(1)}, f32[128,128]{1,0:T(8,128)S(1)}, f32[2,64,128]{2,1,0:T(8,128)S(1)}, f32[2,256,128]{2,1,0:T(8,128)S(1)}) custom-call(bf16[768,4096]{1,0:T(8,128)(2,1)S(1)} %copy-done, bf16[768,1024]{1,0:T(8,128)(2,1)S(1)} %copy-done.1, f32[128,1024]{1,0:T(8,128)S(1)} %copy-done.2, f32[2,64,512]{2,1,0:T(8,128)S(1)} %copy-done.6), custom_call_target="tpu_custom_call" | custom-call | tf_op jit(solution)/shard_map/pallas_call | solution.py:341
  106.8 0.0 copy-done.3
  106.8 0.0 copy-done.4
  106.8 0.0 copy-done.5
  106.8 3.0 %shard_map.111 = (f32[128,1024]{1,0:T(8,128)}, f32[128,1024]{1,0:T(8,128)}, f32[128,1024]{1,0:T(8,128)}, f32[128,1024]{1,0:T(8,128)}, f32[2,64,512]{2,1,0:T(8,128)}) custom-call(f32[128,1024]{1,0:T(8,128)S(1)} %get-tuple-element.9.corr, f32[128,128]{1,0:T(8,128)S(1)} %get-tuple-element.10.pt, f32[2,64,128]{2,1,0:T(8,128)S(1)} %get-tuple-element.11.linv, ...), custom_call_target="tpu_custom_call" | custom-call | tf_op jit(solution)/shard_map/pallas_call | solution.py:390
Async XLA Ops:
  0.6 2.8 %copy-start = (bf16[768,4096]{1,0:T(8,128)(2,1)S(1)}, bf16[768,4096]{1,0:T(8,128)(2,1)}, u32[]{:S(2)}) copy-start(bf16[768,4096]{1,0:T(8,128)(2,1)} %acts.1) | copy-start | bytes 18874372
  3.4 1.4 %copy-start.1 = (bf16[768,1024]{1,0:T(8,128)(2,1)S(1)}, bf16[768,1024]{1,0:T(8,128)(2,1)}, u32[]{:S(2)}) copy-start(bf16[768,1024]{1,0:T(8,128)(2,1)} %cots.1) | copy-start | bytes 4718596
  4.8 1.0 copy-start.2
  5.9 0.9 copy-start.6
  6.8 100.0 %copy-start.3 = (f32[128,1024]{1,0:T(8,128)S(1)}, f32[128,1024]{1,0:T(8,128)}, u32[]{:S(2)}) copy-start(f32[128,1024]{1,0:T(8,128)} %weights.1) | copy-start | bytes 1572868
  6.8 100.0 %copy-start.4 = (f32[128,1024]{1,0:T(8,128)S(1)}, f32[128,1024]{1,0:T(8,128)}, u32[]{:S(2)}) copy-start(f32[128,1024]{1,0:T(8,128)} %first.1) | copy-start | bytes 1572868
  6.8 100.0 %copy-start.5 = (f32[128,1024]{1,0:T(8,128)S(1)}, f32[128,1024]{1,0:T(8,128)}, u32[]{:S(2)}) copy-start(f32[128,1024]{1,0:T(8,128)} %second.1) | copy-start | bytes 1572868

commit v2 on v1

--- a/solution.py
+++ b/solution.py
@@ -14,8 +14,8 @@
 
 F32 = jnp.float32
 BF16 = jnp.bfloat16
-RING = 4
 DEPTH = 8
+SPAN = 174.0
 OFFSETS = (2, 1, 3, 0)
 
 
@@ -25,6 +25,27 @@
 
 def dot_n(a, b):
     return jnp.dot(a, b, precision=highest, preferred_element_type=F32)
+
+
+def encode(source, code):
+    tiles = [slice(128 * i, 128 * (i + 1)) for i in range(4)]
+    top = jnp.abs(source[tiles[0], :])
+    for tile in tiles[1:]:
+        top = jnp.maximum(top, jnp.abs(source[tile, :]))
+    top = jnp.maximum(jnp.max(top, axis=0, keepdims=True) * 1.004, 1e-30).astype(BF16)
+    code[512:528, :] = jnp.broadcast_to(top, (16, 128))
+    scale = SPAN / top.astype(F32)
+    for tile in tiles:
+        value = source[tile, :]
+        size = jnp.exp(jnp.abs(value) * scale - 0.5 * SPAN)
+        code[tile, :] = jnp.where(value < 0.0, -size, size).astype(BF16)
+
+
+def decode(code, tile):
+    scale = code[512:528, :].astype(F32)[0:1] * (1.0 / SPAN)
+    value = code[tile, :].astype(F32)
+    size = (jnp.log(jnp.abs(value)) + 0.5 * SPAN) * scale
+    return jnp.where(value < 0.0, -size, size)
 
 
 class Wire:
@@ -60,8 +81,8 @@
 def kernel_a(
     acts, cots, err, warm,
     corr_out, pt_out, linv_out, n_out,
-    acts_v, cots_v, cots_t, own, rel_a, rel_b, from_m, from_p, rel2_a, rel2_b, from2_m, from2_p,
-    err_v, warm_v, m_t, pt_loc, zr, zsum, n_loc, n_rx, g_loc, g_rx, ns, ra, na, rb, nb, zs, nz, na2, ga, gb, g_half, g_all,
+    acts_v, cots_v, cots_t, own, tx, rx,
+    err_v, warm_v, pt_loc, zr, zsum, n_loc, n_rx, g_loc, g_rx, ns, ra, nb, zs, nz, ga, gb, g_half, g_all,
     t_mat, send_sem, recv_sem, loc_sem,
 ):
     z = lax.axis_index("replica")
@@ -107,7 +128,7 @@
         acts_here[0][s] = local.start(acts.at[:, own_cols(0, s)], acts_v.at[0, pl.ds(0, tokens), pl.ds(128 * s, 128)])
 
     barrier = pltpu.get_barrier_semaphore()
-    friends = [partner] + [along_a(k) for k in (1, 2, 3)] + [along_b(k) for k in (1, 2, 3)] + [along_z(k) for k in range(1, DEPTH)]
+    friends = [partner] + [at(p + i, q + j) for i in range(4) for j in range(4) if i or j] + [along_z(k) for k in range(1, DEPTH)]
     for friend in friends:
         pl.semaphore_signal(barrier, inc=1, device_id=friend, device_id_type=pl.DeviceIdType.MESH)
     pl.semaphore_wait(barrier, len(friends))
@@ -146,29 +167,44 @@
             for s in range(4):
                 own[t, s, rows, :] = part[:, 128 * s:128 * (s + 1)]
 
+    slots = []
+
+    def ship(source, device):
+        i = len(slots)
+        encode(source, tx.at[i])
+        slots.append(wire.start(tx.at[i], rx.at[i], device))
+        return i
+
+    def absorb(target, *arrived):
+        for i in arrived:
+            slots[i].wait_recv()
+        for i in range(4):
+            tile = slice(128 * i, 128 * (i + 1))
+            total = target[tile, :]
+            for slot in arrived:
+                total = total + decode(rx.at[slot], tile)
+            target[tile, :] = total
+
     lo, hi = pl.ds(0, 512), pl.ds(512, 512)
     relay_a, relay_b, outer_m, outer_p, inner_m, inner_p = ([None] * 4 for _ in range(6))
 
     def send_relay(t):
-        relay_a[t] = wire.start(own.at[t, 0, lo], rel_a.at[t], along_a(1))
-        relay_b[t] = wire.start(own.at[t, 0, hi], rel_b.at[t], along_a(3))
+        relay_a[t] = ship(own.at[t, 0, lo], along_a(1))
+        relay_b[t] = ship(own.at[t, 0, hi], along_a(3))
 
     def send_outer(t):
-        outer_m[t] = wire.start(own.at[t, 1, hi], from_m.at[t, hi], along_a(1))
-        outer_p[t] = wire.start(own.at[t, 2, lo], from_p.at[t, lo], along_a(3))
+        outer_m[t] = ship(own.at[t, 1, hi], along_a(1))
+        outer_p[t] = ship(own.at[t, 2, lo], along_a(3))
 
     def send_inner(t):
-        relay_a[t].wait_recv()
-        own[t, 1, lo, :] += rel_a[t]
-        inner_m[t] = wire.start(own.at[t, 1, lo], from_m.at[t, lo], along_a(1))
-        relay_b[t].wait_recv()
-        own[t, 2, hi, :] += rel_b[t]
-        inner_p[t] = wire.start(own.at[t, 2, hi], from_p.at[t, hi], along_a(3))
+        absorb(own.at[t, 1, lo], relay_a[t])
+        inner_m[t] = ship(own.at[t, 1, lo], along_a(1))
+        absorb(own.at[t, 2, hi], relay_b[t])
+        inner_p[t] = ship(own.at[t, 2, hi], along_a(3))
 
     def gather(t):
-        for copy in (outer_m[t], outer_p[t], inner_m[t], inner_p[t]):
-            copy.wait_recv()
-        own[t, 3] += from_m[t] + from_p[t]
+        absorb(own.at[t, 3, lo], outer_p[t], inner_m[t])
+        absorb(own.at[t, 3, hi], outer_m[t], inner_p[t])
 
     compute(0)
     send_relay(0)
@@ -182,31 +218,28 @@
     send_inner(1)
     send_outer(2)
     gather(0)
-    second_a = wire.start(own.at[0, 3, lo], rel2_a, along_b(1))
-    second_b = wire.start(own.at[0, 3, hi], rel2_b, along_b(3))
+    second_a = ship(own.at[0, 3, lo], along_b(1))
+    second_b = ship(own.at[0, 3, hi], along_b(3))
     compute(3)
     send_relay(3)
     send_inner(2)
     send_outer(3)
     gather(1)
-    outer2_m = wire.start(own.at[1, 3, hi], from2_m.at[hi], along_b(1))
-    second_a.wait_recv()
-    own[1, 3, lo, :] += rel2_a[...]
-    inner2_m = wire.start(own.at[1, 3, lo], from2_m.at[lo], along_b(1))
+    outer2_m = ship(own.at[1, 3, hi], along_b(1))
+    absorb(own.at[1, 3, lo], second_a)
+    inner2_m = ship(own.at[1, 3, lo], along_b(1))
     send_inner(3)
     gather(2)
-    outer2_p = wire.start(own.at[2, 3, lo], from2_p.at[lo], along_b(3))
-    second_b.wait_recv()
-    own[2, 3, hi, :] += rel2_b[...]
-    inner2_p = wire.start(own.at[2, 3, hi], from2_p.at[hi], along_b(3))
+    outer2_p = ship(own.at[2, 3, lo], along_b(3))
+    absorb(own.at[2, 3, hi], second_b)
+    inner2_p = ship(own.at[2, 3, hi], along_b(3))
 
     err_copy.wait()
     for i in range(8):
-        m_t[128 * i:128 * (i + 1), :] = err_v[:, 128 * i:128 * (i + 1)].T
-    gather(3)
-    for copy in (outer2_m, inner2_m, outer2_p, inner2_p):
-        copy.wait_recv()
-    m_t[...] += own[3, 3] + (from2_m[...] + from2_p[...])
+        own[3, 3, 128 * i:128 * (i + 1), :] += err_v[:, 128 * i:128 * (i + 1)].T
+    m_t = own.at[3, 3]
+    absorb(own.at[3, 3, lo], outer_p[3], inner_m[3], outer2_p, inner2_m)
+    absorb(own.at[3, 3, hi], outer_m[3], inner_p[3], outer2_m, inner2_p)
 
     warm_copy.wait()
     for j in range(2):
@@ -247,27 +280,27 @@
     n_swap.wait_recv()
     ns[...] = n_loc[c] + n_rx[...]
 
-    def rows_of(index, size):
-        return pl.ds(pl.multiple_of((index % 4) * size, size), size)
-
-    ra_copies = [wire.start(ns.at[rows_of(p + k, 64)], ra.at[k], along_a(k)) for k in (1, 2, 3)]
+    def block(i, j):
+        return pl.ds(pl.multiple_of((((p + i) % 4) * 4 + (q + j) % 4) * 16, 16), 16)
+
+    others = [(i, j) for i in range(4) for j in range(4) if i or j]
+    ra_copies = [wire.start(ns.at[block(i, j)], ra.at[4 * i + j], at(p + i, q + j)) for i, j in others]
     for copy in ga_copies:
         copy.wait_recv()
     gb[q] = (ga[0] + ga[1]) + (ga[2] + ga[3])
     gb_copies = [wire.start(gb.at[q], gb.at[q], along_b(k)) for k in (1, 2, 3)]
-    for copy in ra_copies:
-        copy.wait_recv()
-    na[...] = (ns[rows_of(p, 64), :] + ra[1]) + (ra[2] + ra[3])
-    rb_copies = [wire.start(na.at[rows_of(q + k, 16)], rb.at[k], along_b(k)) for k in (1, 2, 3)]
     for copy in gb_copies:
         copy.wait_recv()
     g_part = (gb[0] + gb[1]) + (gb[2] + gb[3])
     g_half[...] = g_part
     g_all[half, :] = g_part
     g_back = wire.start(g_half, g_all.at[half], partner)
-    for copy in rb_copies:
-        copy.wait_recv()
-    nb[...] = (na[rows_of(q, 16), :] + rb[1]) + (rb[2] + rb[3])
+    for copy in ra_copies:
+        copy.wait_recv()
+    total = ns[block(0, 0), :]
+    for i, j in others:
+        total = total + ra[4 * i + j]
+    nb[...] = total
     zs_copies = [wire.start(nb, zs.at[z], along_z(k)) for k in range(1, DEPTH)]
     zs[z] = nb[...]
 
@@ -295,15 +328,10 @@
     for copy in zs_copies:
         copy.wait_recv()
     nz[...] = ((zs[0] + zs[1]) + (zs[2] + zs[3])) + ((zs[4] + zs[5]) + (zs[6] + zs[7]))
-    back_b = [wire.start(nz, na2.at[rows_of(q, 16)], along_b(k)) for k in (1, 2, 3)]
-    na2[rows_of(q, 16), :] = nz[...]
-    eliminate(20, 35)
-    for copy in back_b:
-        copy.wait_recv()
-    back_a = [wire.start(na2, n_out.at[c, rows_of(p, 64)], along_a(k)) for k in (1, 2, 3)]
-    n_out[c, rows_of(p, 64), :] = na2[...]
-    eliminate(35, 50)
-    for copy in back_a:
+    back = [wire.start(nz, n_out.at[c, block(0, 0)], at(p + i, q + j)) for i, j in others]
+    n_out[c, block(0, 0), :] = nz[...]
+    eliminate(20, 50)
+    for copy in back:
         copy.wait_recv()
     back_c = wire.start(n_out.at[c], n_out.at[c], partner)
     eliminate(50, 64)
@@ -336,7 +364,7 @@
     rows, cols = error_buffer.shape
     shape = jax.ShapeDtypeStruct
     vmem = pl.BlockSpec(memory_space=pltpu.VMEM)
-    anywhere = pl.BlockSpec(memory_space=pl.ANY)
+    anywhere = pl.BlockSpec(memory_space=pltpu.HBM)
     copies = 120
     corr, pt, linv, n = pl.pallas_call(
         kernel_a,
@@ -348,17 +376,10 @@
             pltpu.VMEM((2, tokens, cols), BF16),
             pltpu.VMEM((cols, 2 * tokens), BF16),
             pltpu.VMEM((4, 4, cols, 128), F32),
-            pltpu.VMEM((4, 512, 128), F32),
-            pltpu.VMEM((4, 512, 128), F32),
-            pltpu.VMEM((4, cols, 128), F32),
-            pltpu.VMEM((4, cols, 128), F32),
-            pltpu.VMEM((512, 128), F32),
-            pltpu.VMEM((512, 128), F32),
-            pltpu.VMEM((cols, 128), F32),
-            pltpu.VMEM((cols, 128), F32),
+            pltpu.VMEM((30, 528, 128), BF16),
+            pltpu.VMEM((30, 528, 128), BF16),
             pltpu.VMEM((rows, cols), F32),
             pltpu.VMEM((2, 64, 512), F32),
-            pltpu.VMEM((cols, 128), F32),
             pltpu.VMEM((128, 128), F32),
             pltpu.VMEM((8, 16, 128), F32),
             pltpu.VMEM((16, 128), F32),
@@ -367,13 +388,10 @@
             pltpu.VMEM((64, 128), F32),
             pltpu.VMEM((64, 128), F32),
             pltpu.VMEM((256, 128), F32),
-            pltpu.VMEM((4, 64, 128), F32),
-            pltpu.VMEM((64, 128), F32),
-            pltpu.VMEM((4, 16, 128), F32),
+            pltpu.VMEM((16, 16, 128), F32),
             pltpu.VMEM((16, 128), F32),
             pltpu.VMEM((8, 16, 128), F32),
             pltpu.VMEM((16, 128), F32),
-            pltpu.VMEM((64, 128), F32),
             pltpu.VMEM((4, 32, 128), F32),
             pltpu.VMEM((4, 32, 128), F32),
             pltpu.VMEM((32, 128), F32),
@@ -384,7 +402,7 @@
             pltpu.SemaphoreType.DMA((24,)),
         ],
         compiler_params=pltpu.CompilerParams(
-            collective_id=0, has_side_effects=True, vmem_limit_bytes=44 * 1024 * 1024),
+            collective_id=0, has_side_effects=True, vmem_limit_bytes=60 * 1024 * 1024),
     )(activations, cotangents, error_buffer, warm_factor)
     tile = shape((rows, cols), F32)
     return pl.pallas_call(

time: 110 us -> 88.1 us (0.80)
  Pallas kernels: 103 us -> 83.5 us
  local copies, waits for them, and re-layouts: 6.19 us -> 3.67 us
    pallas_call x1, Pallas kernels: 100 us -> 80.5 us  [local(): pl.pallas_call(kernel_a, out_shape=(shape((rows, cols), F32), shape((128,...]
    unnamed x14, local copies, waits for them, and re-layouts: 6.19 us -> 3.67 us
where the time goes in v2:
time: 88.1 us; the launch traced here: 87.9 us
  Pallas kernels  83.5 us (95%)
  local copies, waits for them, and re-layouts  3.67 us (4%)
    pallas_call x1, Pallas kernels, local(): pl.pallas_call(kernel_a, out_shape=(shape((rows, cols), F32), shape((128,...  80.5 us
    unnamed x14, local copies, waits for them, and re-layouts  3.67 us
    pallas_call x1, Pallas kernels, local(): pl.pallas_call(kernel_b, out_shape=(tile, tile, tile, tile, shape(warm_fa...  2.99 us

profile of v2, /device:TPU:1, one launch (start us, length us, event | category | flops | bytes accessed | tf_op | source)
XLA Modules:
  0.0 87.9 jit_solution(1779118686696038928)
XLA Ops:
  0.6 0.0 copy-start.2
  0.6 0.0 copy-start.1
  0.7 0.0 copy-start
  0.7 80.5 %shard_map.110 = (f32[128,1024]{1,0:T(8,128)}, f32[128,128]{1,0:T(8,128)}, f32[2,64,128]{2,1,0:T(8,128)}, f32[2,256,128]{2,1,0:T(8,128)}) custom-call(bf16[768,4096]{1,0:T(8,128)(2,1)} %acts.1, bf16[768,1024]{1,0:T(8,128)(2,1)} %cots.1, f32[128,1024]{1,0:T(8,128)} %err.1, f32[2,64,512]{2,1,0:T(8,128)} %warm.1), custom_call_target="tpu_custom_call" | custom-call | tf_op jit(solution)/shard_map/pallas_call | solution.py:369
  81.2 0.0 copy-done.2
  81.2 0.0 copy-done.1
  81.2 0.0 copy-done
  81.2 0.0 copy-start.3
  81.2 1.0 %copy-done.3 = f32[128,1024]{1,0:T(8,128)S(1)} copy-done((f32[128,1024]{1,0:T(8,128)S(1)}, f32[128,1024]{1,0:T(8,128)}, u32[]{:S(2)}) %copy-start.3) | copy-done | bytes 524312
  82.2 0.0 copy-start.4
  82.2 0.9 %copy-done.4 = f32[2,256,128]{2,1,0:T(8,128)S(1)} copy-done((f32[2,256,128]{2,1,0:T(8,128)S(1)}, f32[2,256,128]{2,1,0:T(8,128)}, u32[]{:S(2)}) %copy-start.4) | copy-done | bytes 262168
  83.2 0.0 copy-start.5
  83.2 0.8 copy-done.5
  84.0 0.0 copy-start.6
  84.0 0.8 copy-done.6
  84.9 3.0 %shard_map.111 = (f32[128,1024]{1,0:T(8,128)}, f32[128,1024]{1,0:T(8,128)}, f32[128,1024]{1,0:T(8,128)}, f32[128,1024]{1,0:T(8,128)}, f32[2,64,512]{2,1,0:T(8,128)}) custom-call(f32[128,1024]{1,0:T(8,128)S(1)} %copy-done.3, f32[128,128]{1,0:T(8,128)S(1)} %copy-done.5, f32[2,64,128]{2,1,0:T(8,128)S(1)} %copy-done.6, f32[2,256,128]{2,1,0:T(8,128)S(1)} %copy-done.4, ...), custom_call_target="tpu_custom_call" | custom-call | tf_op jit(solution)/shard_map/pallas_call | solution.py:408
Async XLA Ops:
  0.6 80.5 %copy-start.2 = (f32[128,1024]{1,0:T(8,128)S(1)}, f32[128,1024]{1,0:T(8,128)}, u32[]{:S(2)}) copy-start(f32[128,1024]{1,0:T(8,128)} %second.1) | copy-start | bytes 1572868
  0.6 80.5 %copy-start.1 = (f32[128,1024]{1,0:T(8,128)S(1)}, f32[128,1024]{1,0:T(8,128)}, u32[]{:S(2)}) copy-start(f32[128,1024]{1,0:T(8,128)} %first.1) | copy-start | bytes 1572868
  0.7 80.5 %copy-start = (f32[128,1024]{1,0:T(8,128)S(1)}, f32[128,1024]{1,0:T(8,128)}, u32[]{:S(2)}) copy-start(f32[128,1024]{1,0:T(8,128)} %weights.1) | copy-start | bytes 1572868
  81.2 1.0 %copy-start.3 = (f32[128,1024]{1,0:T(8,128)S(1)}, f32[128,1024]{1,0:T(8,128)}, u32[]{:S(2)}) copy-start(f32[128,1024]{1,0:T(8,128)} %get-tuple-element.9.corr) | copy-start | bytes 1572868
  82.2 0.9 %copy-start.4 = (f32[2,256,128]{2,1,0:T(8,128)S(1)}, f32[2,256,128]{2,1,0:T(8,128)}, u32[]{:S(2)}) copy-start(f32[2,256,128]{2,1,0:T(8,128)} %get-tuple-element.12.n) | copy-start | bytes 786436
  83.2 0.8 copy-start.5
  84.0 0.8 copy-start.6

commit v3 on v2

--- a/solution.py
+++ b/solution.py
@@ -50,7 +50,7 @@
 
 class Wire:
     def __init__(self, send, recv):
-        self.send, self.recv, self.copies = send, recv, []
+        self.send, self.recv, self.copies, self.drained = send, recv, [], 0
 
     def start(self, src, dst, device):
         i = len(self.copies)
@@ -63,8 +63,9 @@
         return copy
 
     def drain(self):
-        for copy in self.copies:
+        for copy in self.copies[self.drained:]:
             copy.wait_send()
+        self.drained = len(self.copies)
 
 
 class Local:
@@ -80,10 +81,10 @@
 
 def kernel_a(
     acts, cots, err, warm,
-    corr_out, pt_out, linv_out, n_out,
+    corr_out, basis_out, linv_out, n_out,
     acts_v, cots_v, cots_t, own, tx, rx,
-    err_v, warm_v, pt_loc, zr, zsum, n_loc, n_rx, g_loc, g_rx, ns, ra, nb, zs, nz, ga, gb, g_half, g_all,
-    t_mat, send_sem, recv_sem, loc_sem,
+    err_v, warm_v, corr_v, pt_loc, zr, zsum, n_loc, n_rx, g_loc, g_rx, ns, ra, nb, zs, nz, ga, gb, g_half, g_all,
+    t_mat, pt_v, basis_v, n_v, send_sem, recv_sem, loc_sem,
 ):
     z = lax.axis_index("replica")
     dp = lax.axis_index("dp")
@@ -133,39 +134,47 @@
         pl.semaphore_signal(barrier, inc=1, device_id=friend, device_id_type=pl.DeviceIdType.MESH)
     pl.semaphore_wait(barrier, len(friends))
 
-    cots_there = wire.start(cots, cots_v.at[1], partner)
-    for t in range(4):
+    lo, hi = pl.ds(0, 512), pl.ds(512, 512)
+
+    def swap_acts(t, s):
+        acts_there[t][s] = wire.start(
+            acts.at[:, partner_cols(t, s)], acts_v.at[t, pl.ds(tokens, tokens), pl.ds(128 * s, 128)], partner)
+
+    swap_acts(0, 0)
+    cots_there = [wire.start(cots.at[:, part], cots_v.at[1, :, part], partner) for part in (lo, hi)]
+    for s in (1, 2, 3):
+        swap_acts(0, s)
+    for t in (1, 2, 3):
         for s in range(4):
-            if t > 0:
-                acts_here[t][s] = local.start(
-                    acts.at[:, own_cols(t, s)], acts_v.at[t, pl.ds(0, tokens), pl.ds(128 * s, 128)])
-            acts_there[t][s] = wire.start(
-                acts.at[:, partner_cols(t, s)], acts_v.at[t, pl.ds(tokens, tokens), pl.ds(128 * s, 128)], partner)
+            acts_here[t][s] = local.start(
+                acts.at[:, own_cols(t, s)], acts_v.at[t, pl.ds(0, tokens), pl.ds(128 * s, 128)])
+            swap_acts(t, s)
     err_copy = local.start(err, err_v)
     warm_copy = local.start(warm, warm_v)
 
-    def turn(h):
-        @pl.loop(0, 8)
+    def turn(h, j):
+        @pl.loop(4 * j, 4 * j + 4)
         def _(i):
             cols = pl.ds(pl.multiple_of(i * 128, 128), 128)
             cots_t[cols, h * tokens:(h + 1) * tokens] = cots_v[h, :, cols].T
 
-    cots_here.wait()
-    turn(0)
-    cots_there.wait_recv()
-    turn(1)
-
-    def compute(t):
-        for s in range(4):
+    def product(t, first, last, j):
+        @pl.loop(2 * j, 2 * j + 2)
+        def _(i):
+            rows = pl.ds(pl.multiple_of(i * 256, 256), 256)
+            part = jnp.dot(cots_t[rows, :], acts_v[t, :, 128 * first:128 * last], preferred_element_type=F32)
+            for s in range(first, last):
+                own[t, s, rows, :] = part[:, 128 * (s - first):128 * (s - first + 1)]
+
+    def arrive(t, *blocks):
+        for s in blocks:
             acts_here[t][s].wait()
             acts_there[t][s].wait_recv()
 
-        @pl.loop(0, 4)
-        def _(i):
-            rows = pl.ds(pl.multiple_of(i * 256, 256), 256)
-            part = jnp.dot(cots_t[rows, :], acts_v[t], preferred_element_type=F32)
-            for s in range(4):
-                own[t, s, rows, :] = part[:, 128 * s:128 * (s + 1)]
+    def compute(t):
+        arrive(t, 0, 1, 2, 3)
+        product(t, 0, 4, 0)
+        product(t, 0, 4, 1)
 
     slots = []
 
@@ -185,7 +194,6 @@
                 total = total + decode(rx.at[slot], tile)
             target[tile, :] = total
 
-    lo, hi = pl.ds(0, 512), pl.ds(512, 512)
     relay_a, relay_b, outer_m, outer_p, inner_m, inner_p = ([None] * 4 for _ in range(6))
 
     def send_relay(t):
@@ -206,9 +214,26 @@
         absorb(own.at[t, 3, lo], outer_p[t], inner_m[t])
         absorb(own.at[t, 3, hi], outer_m[t], inner_p[t])
 
-    compute(0)
-    send_relay(0)
-    send_outer(0)
+    cots_here.wait()
+    turn(0, 0)
+    turn(0, 1)
+    arrive(0, 0)
+    cots_there[0].wait_recv()
+    turn(1, 0)
+    product(0, 0, 1, 0)
+    relay_a[0] = ship(own.at[0, 0, lo], along_a(1))
+    cots_there[1].wait_recv()
+    turn(1, 1)
+    product(0, 0, 1, 1)
+    relay_b[0] = ship(own.at[0, 0, hi], along_a(3))
+    arrive(0, 1, 2)
+    product(0, 1, 3, 1)
+    outer_m[0] = ship(own.at[0, 1, hi], along_a(1))
+    product(0, 1, 3, 0)
+    outer_p[0] = ship(own.at[0, 2, lo], along_a(3))
+    arrive(0, 3)
+    product(0, 3, 4, 0)
+    product(0, 3, 4, 1)
     compute(1)
     send_relay(1)
     send_inner(0)
@@ -254,14 +279,16 @@
         scatter[k - 1].wait_recv()
         total = total + zr[k]
     zsum[...] = total
-    spread = [wire.start(zsum, pt_out.at[z_rows(z)], along_z(k)) for k in range(1, DEPTH)]
-    pt_out[z_rows(z), :] = total
+    spread = [wire.start(zsum, pt_v.at[z_rows(z)], along_z(k)) for k in range(1, DEPTH)]
+    pt_v[z_rows(z), :] = total
     for i in range(8):
-        corr_out[:, 128 * i:128 * (i + 1)] = m_t[128 * i:128 * (i + 1), :].T
+        corr_v[:, 128 * i:128 * (i + 1)] = m_t[128 * i:128 * (i + 1), :].T
+    corr_copy = local.start(corr_v, corr_out)
+    wire.drain()
     for copy in spread:
         copy.wait_recv()
 
-    pt = pt_out[...]
+    pt = pt_v[...]
     lane = lax.broadcasted_iota(jnp.int32, (64, 128), 1)
     gram = dot_t(pt, pt)
     g_loc[...] = jnp.where(lane < 64, gram[0:64], gram[64:128])
@@ -285,16 +312,12 @@
 
     others = [(i, j) for i in range(4) for j in range(4) if i or j]
     ra_copies = [wire.start(ns.at[block(i, j)], ra.at[4 * i + j], at(p + i, q + j)) for i, j in others]
+
     for copy in ga_copies:
         copy.wait_recv()
     gb[q] = (ga[0] + ga[1]) + (ga[2] + ga[3])
     gb_copies = [wire.start(gb.at[q], gb.at[q], along_b(k)) for k in (1, 2, 3)]
-    for copy in gb_copies:
-        copy.wait_recv()
-    g_part = (gb[0] + gb[1]) + (gb[2] + gb[3])
-    g_half[...] = g_part
-    g_all[half, :] = g_part
-    g_back = wire.start(g_half, g_all.at[half], partner)
+
     for copy in ra_copies:
         copy.wait_recv()
     total = ns[block(0, 0), :]
@@ -304,59 +327,109 @@
     zs_copies = [wire.start(nb, zs.at[z], along_z(k)) for k in range(1, DEPTH)]
     zs[z] = nb[...]
 
+    for copy in gb_copies:
+        copy.wait_recv()
+    g_part = (gb[0] + gb[1]) + (gb[2] + gb[3])
+    g_half[...] = g_part
+    g_all[half, :] = g_part
+    g_back = wire.start(g_half, g_all.at[half], partner)
+
     g_back.wait_recv()
     row = lax.broadcasted_iota(jnp.int32, (64, 128), 0)
     g = g_all[...]
     eye = jnp.where(lane == row, 1.0, 0.0).astype(F32)
     t_mat[0] = jnp.where(lane >= 64, pltpu.roll(g, 64, 1), eye)
     t_mat[1] = jnp.where(lane >= 64, g, eye)
+    row8 = lax.broadcasted_iota(jnp.int32, (8, 128), 0)
 
     def eliminate(first, last):
-        for k in range(first, last):
-            base = 8 * (k // 8)
-            below = lax.broadcasted_iota(jnp.int32, (64 - base, 1), 0) > k - base
-            for j in range(2):
-                pivot_row = t_mat[j, k:k + 1, :]
-                inv = 1.0 / jnp.sqrt(pivot_row[:, 64 + k:65 + k])
-                scaled = pivot_row * inv
-                column = t_mat[j, base:64, 64 + k:65 + k] * inv
-                column = jnp.where(below, column, 0.0)
-                t_mat[j, base:64, :] -= column * scaled
-                t_mat[j, k:k + 1, :] = scaled
-
-    eliminate(0, 20)
+        low = first // 8
+        mats = [[t_mat[j, 8 * i:8 * (i + 1), :] for i in range(low, 8)] for j in range(2)]
+        for k in range(first, last, 2):
+            top, sub = k // 8 - low, k % 8
+            for mat in mats:
+                left = [jnp.broadcast_to(part[:, 64 + k:65 + k], (8, 128)) for part in mat[top:]]
+                right = [jnp.broadcast_to(part[:, 65 + k:66 + k], (8, 128)) for part in mat[top:]]
+                one, two = mat[top][sub:sub + 1], mat[top][sub + 1:sub + 2]
+                inv_one = 1.0 / left[0][sub:sub + 1]
+                cross = right[0][sub:sub + 1]
+                ratio = left[0][sub + 1:sub + 2] * inv_one
+                two = two - ratio * one
+                inv_two = 1.0 / (right[0][sub + 1:sub + 2] - ratio * cross)
+                for i in range(len(left)):
+                    by_one = left[i] * inv_one
+                    by_two = (right[i] - by_one * cross) * inv_two
+                    if i == 0:
+                        by_one = jnp.where(row8 > sub, by_one, 0.0)
+                        by_two = jnp.where(row8 > sub + 1, by_two, 0.0)
+                    mat[top + i] = mat[top + i] - by_one * one - by_two * two
+        for j in range(2):
+            for i in range(low, 8):
+                t_mat[j, 8 * i:8 * (i + 1), :] = mats[j][i - low]
+
+    eliminate(0, 24)
     for copy in zs_copies:
         copy.wait_recv()
     nz[...] = ((zs[0] + zs[1]) + (zs[2] + zs[3])) + ((zs[4] + zs[5]) + (zs[6] + zs[7]))
-    back = [wire.start(nz, n_out.at[c, block(0, 0)], at(p + i, q + j)) for i, j in others]
-    n_out[c, block(0, 0), :] = nz[...]
-    eliminate(20, 50)
+    back = [wire.start(nz, n_v.at[c, block(0, 0)], at(p + i, q + j)) for i, j in others]
+    n_v[c, block(0, 0), :] = nz[...]
+    eliminate(24, 64)
     for copy in back:
         copy.wait_recv()
-    back_c = wire.start(n_out.at[c], n_out.at[c], partner)
-    eliminate(50, 64)
-    linv_out[...] = t_mat[...]
+    back_c = wire.start(n_v.at[c], n_v.at[c], partner)
+    n_copy = local.start(n_v.at[c], n_out.at[c])
+    for j in range(2):
+        for i in range(8):
+            rows = slice(8 * i, 8 * (i + 1))
+            part = t_mat[j, rows, :]
+            diagonal = jnp.sum(jnp.where(lane[rows] == row[rows] + 64, part, 0.0), axis=1, keepdims=True)
+            t_mat[j, rows, :] = part / jnp.sqrt(diagonal)
+    linv_copy = local.start(t_mat, linv_out)
+    for j in range(2):
+        basis_v[64 * j:64 * (j + 1), :] = dot_n(t_mat[j, :, 0:64], pt[64 * j:64 * (j + 1)])
+    basis_copy = local.start(basis_v, basis_out)
     back_c.wait_recv()
+    n_rest = local.start(n_v.at[1 - c], n_out.at[1 - c])
     wire.drain()
-
-
-def kernel_b(corr, pt, linv, n, weights, first, second, w_out, first_out, second_out, err_out, factor_out):
+    for copy in (corr_copy, n_copy, linv_copy, basis_copy, n_rest):
+        copy.wait()
+
+
+def kernel_b(
+    corr, basis, linv, n, weights, first, second,
+    w_out, first_out, second_out, err_out, factor_out,
+    corr_v, basis_v, linv_v, n_v, weights_v, first_v, second_v, w_new, first_new, second_new, err_new, factor_new, sems,
+):
+    local = Local(sems)
+    small = [local.start(a, b) for a, b in ((linv, linv_v), (n, n_v), (basis, basis_v))]
+    large = [local.start(a, b) for a, b in ((corr, corr_v), (first, first_v), (second, second_v), (weights, weights_v))]
+    for copy in small:
+        copy.wait()
+    bases = []
+    stores = []
     for j in range(2):
-        inverse = linv[j][:, 0:64]
-        basis = dot_n(inverse, pt[64 * j:64 * (j + 1), :]).T
+        inverse = linv_v[j][:, 0:64]
+        bases.append(basis_v[64 * j:64 * (j + 1), :].T)
         for i in range(4):
-            cols = slice(512 * j + 128 * i, 512 * j + 128 * (i + 1))
-            factor = dot_n(inverse, n[j, 64 * i:64 * (i + 1), :]) * 0.125
-            factor_out[j, :, 128 * i:128 * (i + 1)] = factor
-            approx = dot_n(basis, factor)
-            err_out[:, cols] = corr[:, cols] - approx
-            new_first = first_decay * first[:, cols] + (1.0 - first_decay) * approx
-            new_second = second_decay * second[:, cols] + (1.0 - second_decay) * approx * approx
-            first_out[:, cols] = new_first
-            second_out[:, cols] = new_second
-            first_hat = new_first / (1.0 - first_decay**step_count)
-            second_hat = new_second / (1.0 - second_decay**step_count)
-            w_out[:, cols] = weights[:, cols] - learn_rate * first_hat / (jnp.sqrt(second_hat) + adam_epsilon)
+            factor_new[j, :, 128 * i:128 * (i + 1)] = dot_n(inverse, n_v[j, 64 * i:64 * (i + 1), :]) * 0.125
+        stores.append(local.start(factor_new.at[j], factor_out.at[j]))
+    for copy in large:
+        copy.wait()
+    for i in range(4):
+        j, cols = i // 2, slice(256 * i, 256 * (i + 1))
+        approx = dot_n(bases[j], factor_new[j, :, 256 * (i % 2):256 * (i % 2 + 1)])
+        err_new[:, cols] = corr_v[:, cols] - approx
+        new_first = first_decay * first_v[:, cols] + (1.0 - first_decay) * approx
+        new_second = second_decay * second_v[:, cols] + (1.0 - second_decay) * approx * approx
+        first_new[:, cols] = new_first
+        second_new[:, cols] = new_second
+        first_hat = new_first / (1.0 - first_decay**step_count)
+        second_hat = new_second / (1.0 - second_decay**step_count)
+        w_new[:, cols] = weights_v[:, cols] - learn_rate * first_hat / (jnp.sqrt(second_hat) + adam_epsilon)
+        for a, b in ((err_new, err_out), (first_new, first_out), (second_new, second_out), (w_new, w_out)):
+            stores.append(local.start(a.at[:, pl.ds(256 * i, 256)], b.at[:, pl.ds(256 * i, 256)]))
+    for copy in stores:
+        copy.wait()
 
 
 def local(activations, cotangents, error_buffer, master_weights, first_moment, second_moment, warm_factor):
@@ -366,11 +439,11 @@
     vmem = pl.BlockSpec(memory_space=pltpu.VMEM)
     anywhere = pl.BlockSpec(memory_space=pltpu.HBM)
     copies = 120
-    corr, pt, linv, n = pl.pallas_call(
+    corr, basis, linv, n = pl.pallas_call(
         kernel_a,
         out_shape=(shape((rows, cols), F32), shape((128, 128), F32), shape((2, 64, 128), F32), shape((2, 256, 128), F32)),
         in_specs=[anywhere] * 4,
-        out_specs=(vmem,) * 4,
+        out_specs=(anywhere,) * 4,
         scratch_shapes=[
             pltpu.VMEM((4, 2 * tokens, 512), BF16),
             pltpu.VMEM((2, tokens, cols), BF16),
@@ -380,6 +453,7 @@
             pltpu.VMEM((30, 528, 128), BF16),
             pltpu.VMEM((rows, cols), F32),
             pltpu.VMEM((2, 64, 512), F32),
+            pltpu.VMEM((rows, cols), F32),
             pltpu.VMEM((128, 128), F32),
             pltpu.VMEM((8, 16, 128), F32),
             pltpu.VMEM((16, 128), F32),
@@ -397,9 +471,12 @@
             pltpu.VMEM((32, 128), F32),
             pltpu.VMEM((64, 128), F32),
             pltpu.VMEM((2, 64, 128), F32),
+            pltpu.VMEM((128, 128), F32),
+            pltpu.VMEM((128, 128), F32),
+            pltpu.VMEM((2, 256, 128), F32),
             pltpu.SemaphoreType.DMA((copies,)),
             pltpu.SemaphoreType.DMA((copies,)),
-            pltpu.SemaphoreType.DMA((24,)),
+            pltpu.SemaphoreType.DMA((32,)),
         ],
         compiler_params=pltpu.CompilerParams(
             collective_id=0, has_side_effects=True, vmem_limit_bytes=60 * 1024 * 1024),
@@ -408,10 +485,19 @@
     return pl.pallas_call(
         kernel_b,
         out_shape=(tile, tile, tile, tile, shape(warm_factor.shape, F32)),
-        in_specs=[vmem] * 7,
-        out_specs=(vmem,) * 5,
-        compiler_params=pltpu.CompilerParams(vmem_limit_bytes=16 * 1024 * 1024),
-    )(corr, pt, linv, n, master_weights, first_moment, second_moment)
+        in_specs=[anywhere] * 7,
+        out_specs=(anywhere,) * 5,
+        scratch_shapes=[
+            pltpu.VMEM((rows, cols), F32),
+            pltpu.VMEM((128, 128), F32),
+            pltpu.VMEM((2, 64, 128), F32),
+            pltpu.VMEM((2, 256, 128), F32),
+        ] + [pltpu.VMEM((rows, cols), F32)] * 7 + [
+            pltpu.VMEM(warm_factor.shape, F32),
+            pltpu.SemaphoreType.DMA((25,)),
+        ],
+        compiler_params=pltpu.CompilerParams(vmem_limit_bytes=60 * 1024 * 1024),
+    )(corr, basis, linv, n, master_weights, first_moment, second_moment)
 
 
 def solution(mesh):

time: 88.1 us -> 83.2 us (0.944)
  local copies, waits for them, and re-layouts: 3.67 us -> 0 us
  Pallas kernels: 83.5 us -> 82.2 us
    unnamed x14 -> x0, local copies, waits for them, and re-layouts: 3.67 us -> none
    pallas_call x1, Pallas kernels: 80.5 us -> 78.5 us  [local(): pl.pallas_call(kernel_a, out_shape=(shape((rows, cols), F32), shape((128,...]
where the time goes in v3:
time: 83.2 us; the launch traced here: 83 us
  Pallas kernels  82.2 us (99%)
    pallas_call x1, Pallas kernels, local(): pl.pallas_call(kernel_a, out_shape=(shape((rows, cols), F32), shape((128,...  78.5 us
    pallas_call x1, Pallas kernels, local(): pl.pallas_call(kernel_b, out_shape=(tile, tile, tile, tile, shape(warm_fa...  3.78 us

profile of v3, /device:TPU:1, one launch (start us, length us, event | category | flops | bytes accessed | tf_op | source)
XLA Modules:
  0.0 83.0 jit_solution(9138166106875543237)
XLA Ops:
  0.6 78.5 %shard_map.110 = (f32[128,1024]{1,0:T(8,128)}, f32[128,128]{1,0:T(8,128)}, f32[2,64,128]{2,1,0:T(8,128)}, f32[2,256,128]{2,1,0:T(8,128)}) custom-call(bf16[768,4096]{1,0:T(8,128)(2,1)} %acts.1, bf16[768,1024]{1,0:T(8,128)(2,1)} %cots.1, f32[128,1024]{1,0:T(8,128)} %err.1, f32[2,64,512]{2,1,0:T(8,128)} %warm.1), custom_call_target="tpu_custom_call" | custom-call | tf_op jit(solution)/shard_map/pallas_call | solution.py:442
  79.1 3.8 %shard_map.111 = (f32[128,1024]{1,0:T(8,128)}, f32[128,1024]{1,0:T(8,128)}, f32[128,1024]{1,0:T(8,128)}, f32[128,1024]{1,0:T(8,128)}, f32[2,64,512]{2,1,0:T(8,128)}) custom-call(f32[128,1024]{1,0:T(8,128)} %get-tuple-element.9.corr, f32[128,128]{1,0:T(8,128)} %get-tuple-element.10.basis, f32[2,64,128]{2,1,0:T(8,128)} %get-tuple-element.11.linv, ...), custom_call_target="tpu_custom_call" | custom-call | tf_op jit(solution)/shard_map/pallas_call | solution.py:485

commit v4 on v3

--- a/solution.py
+++ b/solution.py
@@ -84,7 +84,7 @@
     corr_out, basis_out, linv_out, n_out,
     acts_v, cots_v, cots_t, own, tx, rx,
     err_v, warm_v, corr_v, pt_loc, zr, zsum, n_loc, n_rx, g_loc, g_rx, ns, ra, nb, zs, nz, ga, gb, g_half, g_all,
-    t_mat, pt_v, basis_v, n_v, send_sem, recv_sem, loc_sem,
+    t_mat, pt_v, basis_v, n_v, send_sem, recv_sem, loc_sem, news_sem,
 ):
     z = lax.axis_index("replica")
     dp = lax.axis_index("dp")
@@ -129,7 +129,7 @@
         acts_here[0][s] = local.start(acts.at[:, own_cols(0, s)], acts_v.at[0, pl.ds(0, tokens), pl.ds(128 * s, 128)])
 
     barrier = pltpu.get_barrier_semaphore()
-    friends = [partner] + [at(p + i, q + j) for i in range(4) for j in range(4) if i or j] + [along_z(k) for k in range(1, DEPTH)]
+    friends = [partner, along_a(1), along_a(3), along_b(1), along_b(3), along_z(1), along_z(7)]
     for friend in friends:
         pl.semaphore_signal(barrier, inc=1, device_id=friend, device_id_type=pl.DeviceIdType.MESH)
     pl.semaphore_wait(barrier, len(friends))
@@ -151,6 +151,13 @@
             swap_acts(t, s)
     err_copy = local.start(err, err_v)
     warm_copy = local.start(warm, warm_v)
+
+    def tell(index, k):
+        pl.semaphore_signal(
+            news_sem.at[index], inc=1, device_id=along_z(k), device_id_type=pl.DeviceIdType.MESH)
+
+    def hear(index):
+        pl.semaphore_wait(news_sem.at[index], 1)
 
     def turn(h, j):
         @pl.loop(4 * j, 4 * j + 4)
@@ -234,21 +241,43 @@
     arrive(0, 3)
     product(0, 3, 4, 0)
     product(0, 3, 4, 1)
-    compute(1)
+    tell(0, 1)
+    tell(1, 7)
+    arrive(1, 0, 1, 2, 3)
+    product(1, 0, 1, 0)
+    product(1, 0, 1, 1)
     send_relay(1)
     send_inner(0)
+    product(1, 1, 4, 0)
+    product(1, 1, 4, 1)
     send_outer(1)
-    compute(2)
+    hear(0)
+    hear(1)
+    tell(2, 1)
+    tell(3, 7)
+    arrive(2, 0, 1, 2, 3)
+    product(2, 0, 1, 0)
+    product(2, 0, 1, 1)
     send_relay(2)
     send_inner(1)
+    product(2, 1, 4, 0)
+    product(2, 1, 4, 1)
     send_outer(2)
+    hear(2)
+    hear(3)
+    tell(4, 1)
+    arrive(3, 0, 1, 2, 3)
+    product(3, 0, 1, 0)
+    product(3, 0, 1, 1)
+    send_relay(3)
     gather(0)
     second_a = ship(own.at[0, 3, lo], along_b(1))
     second_b = ship(own.at[0, 3, hi], along_b(3))
-    compute(3)
-    send_relay(3)
     send_inner(2)
+    product(3, 1, 4, 0)
+    product(3, 1, 4, 1)
     send_outer(3)
+    hear(4)
     gather(1)
     outer2_m = ship(own.at[1, 3, hi], along_b(1))
     absorb(own.at[1, 3, lo], second_a)
@@ -294,9 +323,9 @@
     g_loc[...] = jnp.where(lane < 64, gram[0:64], gram[64:128])
     g_swap = wire.start(g_loc, g_rx, partner)
     for j in range(2):
+        part = dot_t(pt[64 * j:64 * (j + 1)], m_t[512 * j:512 * (j + 1), :])
         for i in range(4):
-            n_loc[j, 64 * i:64 * (i + 1), :] = dot_t(
-                pt[64 * j:64 * (j + 1)], m_t[512 * j + 128 * i:512 * j + 128 * (i + 1), :])
+            n_loc[j, 64 * i:64 * (i + 1), :] = part[:, 128 * i:128 * (i + 1)]
     n_swap = wire.start(n_loc.at[1 - c], n_rx, partner)
 
     half = pl.ds(pl.multiple_of(c * 32, 32), 32)
@@ -410,8 +439,8 @@
     for j in range(2):
         inverse = linv_v[j][:, 0:64]
         bases.append(basis_v[64 * j:64 * (j + 1), :].T)
-        for i in range(4):
-            factor_new[j, :, 128 * i:128 * (i + 1)] = dot_n(inverse, n_v[j, 64 * i:64 * (i + 1), :]) * 0.125
+        total = jnp.concatenate([n_v[j, 64 * i:64 * (i + 1), :] for i in range(4)], axis=1)
+        factor_new[j] = dot_n(inverse, total) * 0.125
         stores.append(local.start(factor_new.at[j], factor_out.at[j]))
     for copy in large:
         copy.wait()
@@ -477,6 +506,7 @@
             pltpu.SemaphoreType.DMA((copies,)),
             pltpu.SemaphoreType.DMA((copies,)),
             pltpu.SemaphoreType.DMA((32,)),
+            pltpu.SemaphoreType.REGULAR((5,)),
         ],
         compiler_params=pltpu.CompilerParams(
             collective_id=0, has_side_effects=True, vmem_limit_bytes=60 * 1024 * 1024),

time: 83.2 us -> 78.8 us (0.947)
  Pallas kernels: 82.2 us -> 77.8 us
    pallas_call x1, Pallas kernels: 78.5 us -> 74 us  [local(): pl.pallas_call(kernel_a, out_shape=(shape((rows, cols), F32), shape((128,...]
where the time goes in v4:
time: 78.8 us; the launch traced here: 78.6 us
  Pallas kernels  77.8 us (99%)
  between operations  0.8 us (1%)
    pallas_call x1, Pallas kernels, local(): pl.pallas_call(kernel_a, out_shape=(shape((rows, cols), F32), shape((128,...  74 us
    pallas_call x1, Pallas kernels, local(): pl.pallas_call(kernel_b, out_shape=(tile, tile, tile, tile, shape(warm_fa...  3.78 us

profile of v4, /device:TPU:1, one launch (start us, length us, event | category | flops | bytes accessed | tf_op | source)
XLA Modules:
  0.0 78.6 jit_solution(5732687163873762086)
XLA Ops:
  0.6 74.0 %shard_map.110 = (f32[128,1024]{1,0:T(8,128)}, f32[128,128]{1,0:T(8,128)}, f32[2,64,128]{2,1,0:T(8,128)}, f32[2,256,128]{2,1,0:T(8,128)}) custom-call(bf16[768,4096]{1,0:T(8,128)(2,1)} %acts.1, bf16[768,1024]{1,0:T(8,128)(2,1)} %cots.1, f32[128,1024]{1,0:T(8,128)} %err.1, f32[2,64,512]{2,1,0:T(8,128)} %warm.1), custom_call_target="tpu_custom_call" | custom-call | tf_op jit(solution)/shard_map/pallas_call | solution.py:471
  74.7 3.8 %shard_map.111 = (f32[128,1024]{1,0:T(8,128)}, f32[128,1024]{1,0:T(8,128)}, f32[128,1024]{1,0:T(8,128)}, f32[128,1024]{1,0:T(8,128)}, f32[2,64,512]{2,1,0:T(8,128)}) custom-call(f32[128,1024]{1,0:T(8,128)} %get-tuple-element.9.corr, f32[128,128]{1,0:T(8,128)} %get-tuple-element.10.basis, f32[2,64,128]{2,1,0:T(8,128)} %get-tuple-element.11.linv, ...), custom_call_target="tpu_custom_call" | custom-call | tf_op jit(solution)/shard_map/pallas_call | solution.py:515

commit v5 on v4

--- a/solution.py
+++ b/solution.py
@@ -292,12 +292,13 @@
     for i in range(8):
         own[3, 3, 128 * i:128 * (i + 1), :] += err_v[:, 128 * i:128 * (i + 1)].T
     m_t = own.at[3, 3]
-    absorb(own.at[3, 3, lo], outer_p[3], inner_m[3], outer2_p, inner2_m)
-    absorb(own.at[3, 3, hi], outer_m[3], inner_p[3], outer2_m, inner2_p)
-
+    absorb(own.at[3, 3, lo], outer_p[3], inner2_m)
+    absorb(own.at[3, 3, hi], outer_m[3], outer2_m)
     warm_copy.wait()
-    for j in range(2):
-        pt_loc[64 * j:64 * (j + 1), :] = dot_n(warm_v[j], m_t[512 * j:512 * (j + 1), :])
+    absorb(own.at[3, 3, lo], inner_m[3], outer2_p)
+    pt_loc[0:64, :] = dot_n(warm_v[0], m_t[0:512, :])
+    absorb(own.at[3, 3, hi], inner_p[3], inner2_p)
+    pt_loc[64:128, :] = dot_n(warm_v[1], m_t[512:1024, :])
 
     def z_rows(zz):
         return pl.ds(pl.multiple_of((zz % DEPTH) * 16, 16), 16)
@@ -434,27 +435,26 @@
     large = [local.start(a, b) for a, b in ((corr, corr_v), (first, first_v), (second, second_v), (weights, weights_v))]
     for copy in small:
         copy.wait()
-    bases = []
     stores = []
-    for j in range(2):
-        inverse = linv_v[j][:, 0:64]
-        bases.append(basis_v[64 * j:64 * (j + 1), :].T)
-        total = jnp.concatenate([n_v[j, 64 * i:64 * (i + 1), :] for i in range(4)], axis=1)
-        factor_new[j] = dot_n(inverse, total) * 0.125
-        stores.append(local.start(factor_new.at[j], factor_out.at[j]))
-    for copy in large:
-        copy.wait()
     for i in range(4):
         j, cols = i // 2, slice(256 * i, 256 * (i + 1))
-        approx = dot_n(bases[j], factor_new[j, :, 256 * (i % 2):256 * (i % 2 + 1)])
+        if i % 2 == 0:
+            total = jnp.concatenate([n_v[j, 64 * k:64 * (k + 1), :] for k in range(4)], axis=1)
+            factor_new[j] = dot_n(linv_v[j][:, 0:64], total) * 0.125
+            basis_t = basis_v[64 * j:64 * (j + 1), :].T
+            stores.append(local.start(factor_new.at[j], factor_out.at[j]))
+        approx = dot_n(basis_t, factor_new[j, :, 256 * (i % 2):256 * (i % 2 + 1)])
+        if i == 0:
+            for copy in large:
+                copy.wait()
         err_new[:, cols] = corr_v[:, cols] - approx
         new_first = first_decay * first_v[:, cols] + (1.0 - first_decay) * approx
         new_second = second_decay * second_v[:, cols] + (1.0 - second_decay) * approx * approx
         first_new[:, cols] = new_first
         second_new[:, cols] = new_second
-        first_hat = new_first / (1.0 - first_decay**step_count)
-        second_hat = new_second / (1.0 - second_decay**step_count)
-        w_new[:, cols] = weights_v[:, cols] - learn_rate * first_hat / (jnp.sqrt(second_hat) + adam_epsilon)
+        first_hat = new_first * (learn_rate / (1.0 - first_decay**step_count))
+        second_hat = new_second * (1.0 / (1.0 - second_decay**step_count))
+        w_new[:, cols] = weights_v[:, cols] - first_hat / (jnp.sqrt(second_hat) + adam_epsilon)
         for a, b in ((err_new, err_out), (first_new, first_out), (second_new, second_out), (w_new, w_out)):
             stores.append(local.start(a.at[:, pl.ds(256 * i, 256)], b.at[:, pl.ds(256 * i, 256)]))
     for copy in stores:

time: 78.8 us -> 78.7 us (level)
  no operation moved by 1% of the time
where the time goes in v5:
time: 78.7 us; the launch traced here: 78.6 us
  Pallas kernels  77.8 us (99%)
  between operations  0.8 us (1%)
    pallas_call x1, Pallas kernels, local(): pl.pallas_call(kernel_a, out_shape=(shape((rows, cols), F32), shape((128,...  74.2 us
    pallas_call x1, Pallas kernels, local(): pl.pallas_call(kernel_b, out_shape=(tile, tile, tile, tile, shape(warm_fa...  3.63 us

profile of v5, /device:TPU:1, one launch (start us, length us, event | category | flops | bytes accessed | tf_op | source)
XLA Modules:
  0.0 78.6 jit_solution(17926372735950307247)
XLA Ops:
  0.6 74.2 %shard_map.110 = (f32[128,1024]{1,0:T(8,128)}, f32[128,128]{1,0:T(8,128)}, f32[2,64,128]{2,1,0:T(8,128)}, f32[2,256,128]{2,1,0:T(8,128)}) custom-call(bf16[768,4096]{1,0:T(8,128)(2,1)} %acts.1, bf16[768,1024]{1,0:T(8,128)(2,1)} %cots.1, f32[128,1024]{1,0:T(8,128)} %err.1, f32[2,64,512]{2,1,0:T(8,128)} %warm.1), custom_call_target="tpu_custom_call" | custom-call | tf_op jit(solution)/shard_map/pallas_call | solution.py:471
  74.8 3.6 %shard_map.111 = (f32[128,1024]{1,0:T(8,128)}, f32[128,1024]{1,0:T(8,128)}, f32[128,1024]{1,0:T(8,128)}, f32[128,1024]{1,0:T(8,128)}, f32[2,64,512]{2,1,0:T(8,128)}) custom-call(f32[128,1024]{1,0:T(8,128)} %get-tuple-element.9.corr, f32[128,128]{1,0:T(8,128)} %get-tuple-element.10.basis, f32[2,64,128]{2,1,0:T(8,128)} %get-tuple-element.11.linv, ...), custom_call_target="tpu_custom_call" | custom-call | tf_op jit(solution)/shard_map/pallas_call | solution.py:515
